TPU v7x, 512 devices: a whole 4x8x8 slice. The times are simulated.
512 devices in a mesh: shard: 128 (over y, x_lo, z), comp: 2 (over core), band: 2 (over x_hi).
Axes of the slice: x: 4 (x_hi: 2, x_lo: 2; x = x_hi * 2 + x_lo), y: 8, z: 8, core: 2. Of those that a mesh axis runs over, the one named last changes fastest.
Arguments:
- coefficients: float32 [2, 256, 5120], P(None, None, 'shard'), may hold values from -6 to 6
- pair_orders: int32 [128], replicated, may hold values from 1 to 2559, as said below
- legendre: bfloat16 [128, 5120, 512], P('shard', 'band', 'comp'), may hold values from -0.0048828125 to 0.0048828125
- derivative: bfloat16 [2, 128, 5120, 512], P('comp', 'shard', 'band'), may hold values from -0.0048828125 to 0.0048828125
Outputs:
- gradients: float32 [512, 6, 21600], P(('shard', 'band'), 'comp')
Inputs may be any that keep to these rules, and one draw needn't show every extreme that they name: `pair_orders`: distinct values; the smallest and the largest allowed value both occur.
All inputs are finite; a program needn't handle non-finite values.
Results may differ from a plain program's by a relative error of at most 0.0032.
Values may be sent and summed in bfloat16 or wider, within the bound.
No kernel may reach another device: no remote copies, remote signals or barrier semaphores. Data moves between devices by JAX's collectives and lax.ppermute only.
A program may use at most 64 MiB of HBM per device.

v0:
```python
import jax
import jax.numpy as jnp
from jax import lax
from jax.sharding import PartitionSpec as P

DEGS = 5120
NLON = 21600


def cycle_angles(cycle_ids, total):
    return jnp.pi / 4.0 + (cycle_ids.astype(jnp.float32) + 0.5) * (jnp.pi / (2.0 * total))


def order_factors(order_values, sine_values):
    return order_values.astype(jnp.float32) / DEGS / sine_values[..., None]


def degree_weights(degree):
    linear_weight = (degree + 1.0) / DEGS
    shifted_weight = (degree + 2.0) / DEGS
    return (linear_weight * shifted_weight, linear_weight, shifted_weight)


def pack_pair(first_order, second_order, order_value, positions):
    item_count = positions.shape[0]
    split_point = DEGS - order_value
    padded = jnp.concatenate([first_order, jnp.zeros_like(first_order)], axis=1)
    shifted = lax.dynamic_slice_in_dim(padded, order_value + positions[0], item_count, 1)
    second_part = lax.dynamic_slice_in_dim(second_order, positions[0], item_count, 1)
    inside = positions < split_point
    lead_part = jnp.where(inside[None, :], shifted, 0.0)
    tail_part = jnp.where(inside[None, :], 0.0, second_part)
    degree = jnp.where(inside, positions + order_value, positions).astype(jnp.float32)
    return (lead_part, tail_part, degree)


def weighted(lead_part, tail_part, bases):
    both_orders = jnp.stack([lead_part, tail_part], axis=-1)
    scaled_parts = [factor[..., None, :, None] * both_orders for factor in bases]
    stacked = jnp.stack(scaled_parts, axis=-4)
    reordered = jnp.moveaxis(stacked, -2, -4)
    return reordered.reshape(reordered.shape[:-3] + (6, 2)).astype(jnp.bfloat16)


def components(basis_sums, group_zero, cotangent, order_factor):
    zero_cos = basis_sums[..., 0, 0, :]
    zero_sin = basis_sums[..., 0, 1, :]
    one_cos = basis_sums[..., 1, 0, :]
    one_sin = basis_sums[..., 1, 1, :]
    two_cos = basis_sums[..., 2, 0, :]
    two_sin = basis_sums[..., 2, 1, :]
    along_cos = two_cos - one_cos
    along_sin = two_sin - one_sin
    first_set = [
        along_cos,
        along_sin,
        -along_cos - zero_cos,
        -along_sin - zero_sin,
        zero_cos,
        zero_sin,
    ]
    second_set = [
        one_cos + cotangent * zero_cos,
        one_sin + cotangent * zero_sin,
        order_factor * zero_sin,
        -(order_factor * zero_cos),
        order_factor * two_sin,
        -(order_factor * two_cos),
    ]
    chosen = [jnp.where(group_zero, left, right) for left, right in zip(first_set, second_set)]
    return jnp.stack(chosen, axis=-2)


def longitude_tables(order_all):
    blocks = 10
    block_width = NLON // blocks
    offsets = jnp.arange(block_width, dtype=jnp.int32)
    starts = jnp.arange(blocks, dtype=jnp.int32) * block_width
    inner_phase = order_all[:, None] * offsets[None, :] % NLON
    outer_phase = starts[:, None] * order_all[None, :] % NLON
    inner_angle = inner_phase.astype(jnp.float32) * (2.0 * jnp.pi / NLON)
    outer_angle = outer_phase.astype(jnp.float32) * (2.0 * jnp.pi / NLON)
    lon_table = jnp.concatenate([jnp.cos(inner_angle), jnp.sin(inner_angle)], axis=0)
    return (lon_table, jnp.cos(outer_angle), jnp.sin(outer_angle))


def on_device(coefficients, pair_orders, legendre, derivative):
    shard_count = lax.axis_size("shard")
    band_count = lax.axis_size("band")
    group_zero = lax.axis_index("comp") == 0
    band_index = lax.axis_index("band")
    shard_index = lax.axis_index("shard")
    pairs_dev = legendre.shape[0]
    half_rows = legendre.shape[1]
    cycle_total = derivative.shape[3]
    cycle_dev = cycle_total // (shard_count * band_count)
    gathered = lax.all_to_all(coefficients, "shard", split_axis=1, concat_axis=2, tiled=True)
    gathered = gathered.reshape(2, pairs_dev, 2, DEGS)
    own_orders = lax.dynamic_slice_in_dim(pair_orders, shard_index * pairs_dev, pairs_dev)
    positions = band_index * half_rows + jnp.arange(half_rows, dtype=jnp.int32)
    lead_part, tail_part, degree = jax.vmap(pack_pair, in_axes=(1, 1, 0, None))(
        gathered[:, :, 0], gathered[:, :, 1], own_orders, positions
    )
    square_weight, linear_weight, shifted_weight = degree_weights(degree)
    zero_weights = jnp.zeros_like(degree)
    unit_weights = jnp.ones_like(degree)
    t_weights = (zero_weights, jnp.where(group_zero, zero_weights, shifted_weight), unit_weights)
    right_t = weighted(lead_part, tail_part, t_weights)
    table_t = derivative[0]
    a_weights = (
        jnp.where(group_zero, square_weight, shifted_weight),
        jnp.where(group_zero, linear_weight, zero_weights),
        zero_weights,
    )
    right_a = weighted(lead_part, tail_part, a_weights)
    from_values = jnp.einsum(
        "pdr,pdcj->rcpj",
        lax.all_gather(legendre, "comp", axis=2, tiled=True),
        right_a,
        preferred_element_type=jnp.float32,
    )
    from_deriv = jnp.einsum("pdr,pdcj->rcpj", table_t, right_t, preferred_element_type=jnp.float32)
    basis_sums = from_values + from_deriv
    spread = basis_sums.reshape(shard_count, band_count, cycle_dev, 6, pairs_dev * 2)
    kept_sums = lax.psum_scatter(spread, "band", scatter_dimension=1, tiled=True)
    kept_sums = kept_sums.reshape(shard_count, cycle_dev, 3, 2, pairs_dev * 2)
    cycle_ids = (
        jnp.arange(shard_count, dtype=jnp.int32)[:, None] * band_count + band_index
    ) * cycle_dev + jnp.arange(cycle_dev, dtype=jnp.int32)[None, :]
    colatitude = cycle_angles(cycle_ids, cycle_total)
    sine_values = jnp.sin(colatitude)
    cotangent = jnp.cos(colatitude) / sine_values
    local_orders = jnp.stack([own_orders, DEGS - own_orders], axis=1).reshape(-1)
    order_factor = order_factors(local_orders, sine_values)
    spectra = components(kept_sums, group_zero, cotangent[..., None], order_factor)
    order_all = jnp.stack([pair_orders, DEGS - pair_orders], axis=1).reshape(-1)
    lon_table, turn_cos, turn_sin = longitude_tables(order_all)
    pieces = lax.all_to_all(spectra, "shard", split_axis=0, concat_axis=3, tiled=True)
    item_count = pieces.shape[1]
    spectra_in = pieces.reshape(item_count, 3, 2, pieces.shape[3])
    cos_part = spectra_in[:, :, 0, None, :]
    sin_part = spectra_in[:, :, 1, None, :]
    turned_cos = cos_part * turn_cos + sin_part * turn_sin
    turned_sin = sin_part * turn_cos - cos_part * turn_sin
    block_count = turn_cos.shape[0]
    left_side = jnp.concatenate([turned_cos, turned_sin], axis=-1).reshape(
        item_count * 3 * block_count, -1
    )
    fields = jnp.dot(
        left_side, lon_table, precision=lax.Precision.HIGHEST, preferred_element_type=jnp.float32
    )
    return fields.reshape(item_count, 3, NLON)


def solution(mesh):
    placed = (
        P(None, None, "shard"),
        P(),
        P("shard", "band", "comp"),
        P("comp", "shard", "band", None),
    )
    return jax.shard_map(
        on_device,
        mesh=mesh,
        in_specs=placed,
        out_specs=P(("shard", "band"), "comp", None),
        check_vma=False,
    )
```

profile of v0, /device:TPU:8, one launch (start us, length us, event | category | flops | bytes accessed | tf_op | source)
XLA Modules:
  0.0 116.5 jit_solution(3873268857761337029)
XLA Ops:
  6.5 0.7 all-gather.2.cloned.1.call-update
  7.3 1.1 copy.67
  8.4 1.1 reshape.879
  9.4 18.3 %all-to-all-start = ((f32[128,1,160]{2,1,0:T(1,128)}), f32[128,1,160]{2,1,0:T(1,128)S(1)}, u32[]{:S(2)}, u32[]{:S(2)}) async-start(f32[128,1,160]{2,1,0:T(1,128)} %reshape.879), calls=%async_computation | async-start | bytes 262144 | tf_op jit(solution)/shard_map/all_to_all | solution.py:97
  27.8 0.7 dynamic_slice.3
  29.3 0.5 slice.76
  31.3 11.4 %fusion.13 = (f32[256,2160]{1,0:T(8,128)}, f32[256,2160]{1,0:T(8,128)}) fusion(s32[256]{0:T(256)S(1)} %mul.300), kind=kLoop, calls=%fused_computation.15 | loop fusion | flops 4976640 | bytes 4424704 | tf_op jit(solution)/shard_map/cos | solution.py:83
  42.7 0.8 fusion.45
  43.4 0.7 fusion.40
  46.1 0.6 slice.73
  46.8 1.3 %dynamic-slice.9 = u32[1]{0:T(128)} dynamic-slice(u32[512]{0:T(512)} %constant.122, u32[]{:T(128)S(6)} %add.244), dynamic_slice_sizes={1} | dynamic-slice | bytes 12
  48.1 0.7 multiply_select_fusion
  48.8 0.5 broadcast.682
  49.3 1.0 reduce
  50.2 0.3 reshape.880
  50.9 0.8 fusion.26
  51.7 0.8 fusion.28
  52.8 0.5 fusion.4
  53.3 2.2 %fusion.18 = f32[512,6,1,2]{0,1,3,2:T(8,128)S(1)} fusion(f32[6,2,512]{2,0,1:T(8,128)S(1)} %fusion.4, bf16[1,2560,512]{2,1,0:T(8,128)(2,1)} %all-gather.2.cloned.1.call-done, bf16[2560,6,2]{0,2,1:T(2,128)(2,1)S(1)} %bitcast.150), kind=kOutput, calls=%fused_computation.18 | convolution fusion | flops 31463424 | bytes 2732032 | tf_op jit(solution)/shard_map/pdr,pdcj->rcpj/dot_general | solution.py:116
  55.6 0.2 copy.72
  55.8 0.3 copy.73
  56.1 11.1 %all-reduce.1 = f32[128,2,2,6,2]{0,4,3,2,1:T(2,128)S(1)} all-reduce(f32[128,2,2,6,2]{0,4,3,2,1:T(2,128)S(1)} %copy.73), channel_id=2, replica_groups=mesh['shard'=128,'comp'=2,'band'=2] {'band'}, use_global_device_ids=true, to_apply=%region_0.1.clone | all-reduce | flops 6144 | bytes 49152
  67.2 0.6 constant_dynamic-slice_fusion
  68.1 0.9 copy.79
  69.0 14.0 %all-to-all-start.1 = ((f32[128,2,6,2]{2,3,1,0:T(2,128)}), f32[128,2,6,2]{2,3,1,0:T(2,128)S(1)}, u32[]{:S(2)}, u32[]{:S(2)}) async-start(f32[128,2,6,2]{2,3,1,0:T(2,128)} %copy.79), calls=%async_computation.1 | async-start | bytes 524288 | tf_op jit(solution)/shard_map/all_to_all | solution.py:138
  83.2 13.5 %all-to-all-done.1 = f32[128,2,6,2]{2,3,1,0:T(2,128)S(1)} async-done(((f32[128,2,6,2]{2,3,1,0:T(2,128)}), f32[128,2,6,2]{2,3,1,0:T(2,128)S(1)}, u32[]{:S(2)}, u32[]{:S(2)}) %all-to-all-start.1) | async-done | bytes 12320 | tf_op jit(solution)/shard_map/all_to_all | solution.py:138
  96.7 0.7 copy-done.1
  97.4 3.1 %copy.80 = f32[1,2,6,128,2]{4,3,2,1,0:T(8,128)S(1)} copy(f32[1,2,6,128,2]{2,4,1,3,0:T(2,128)} %bitcast.149) | data formatting | bytes 24576 | tf_op jit(solution)/shard_map/all_to_all | solution.py:138
  100.5 0.5 reshape.820
  101.1 5.9 %fusion = f32[60,2160]{1,0:T(8,128)} fusion(f32[256,2160]{1,0:T(8,128)} %get-tuple-element.47, f32[256,2160]{1,0:T(8,128)} %get-tuple-element.46, f32[60,256]{1,0:T(8,128)S(1)} %sub.73, f32[60,256]{1,0:T(8,128)S(1)} %add.237), kind=kOutput, calls=%fused_computation | convolution fusion | flops 797399040 | bytes 5064960 | tf_op jit(solution)/shard_map/dot_general | solution.py:149
  107.0 1.6 %reshape.821 = f32[2,3,21600]{2,1,0:T(4,128)S(1)} reshape(f32[60,2160]{1,0:T(8,128)} %fusion) | data formatting | bytes 1036800 | tf_op jit(solution)/shard_map/reshape | solution.py:152
  108.6 1.1 copy.86
  (40 shorter events, 1.6 us)
Async XLA Ops:
  6.5 46.3 %copy-start = (bf16[1,1,2560,512]{3,2,1,0:T(8,128)(2,1)S(1)}, bf16[1,1,2560,512]{3,2,1,0:T(8,128)(2,1)}, u32[]{:S(2)}) copy-start(bf16[1,1,2560,512]{3,2,1,0:T(8,128)(2,1)} %param.7) | copy-start | bytes 7864324
  6.5 21.3 %copy-start.2 = (s32[128]{0:T(128)S(1)}, s32[128]{0:T(128)}, u32[]{:S(2)}) copy-start(s32[128]{0:T(128)} %param.5) | copy-start | bytes 1540
  6.5 46.8 %all-gather.2.cloned.1.call-start = ((), (), s32[]{:S(2)}) async-start(), calls=%async_computation.2 | async-start | bytes 3932160 | tf_op jit(solution)/shard_map/all_gather | solution.py:118
  9.4 39.3 %all-to-all-start = ((f32[128,1,160]{2,1,0:T(1,128)}), f32[128,1,160]{2,1,0:T(1,128)S(1)}, u32[]{:S(2)}, u32[]{:S(2)}) async-start(f32[128,1,160]{2,1,0:T(1,128)} %reshape.879), calls=%async_computation | async-start | bytes 262144 | tf_op jit(solution)/shard_map/all_to_all | solution.py:97
  69.0 27.7 %all-to-all-start.1 = ((f32[128,2,6,2]{2,3,1,0:T(2,128)}), f32[128,2,6,2]{2,3,1,0:T(2,128)S(1)}, u32[]{:S(2)}, u32[]{:S(2)}) async-start(f32[128,2,6,2]{2,3,1,0:T(2,128)} %copy.79), calls=%async_computation.1 | async-start | bytes 524288 | tf_op jit(solution)/shard_map/all_to_all | solution.py:138
  96.7 0.7 copy-start.1
Sparse Core Ops, SparseCore 0:
  9.4 23.7 all-gather.1
where the time goes:
time: 117 us; the launch traced here: 116 us
  starting transfers between devices  32.3 us (28%)
  between operations  17.6 us (15%)
  other arithmetic  17 us (15%)
  local copies, waits for them, and re-layouts  15.6 us (13%)
  waiting for transfers between devices  14.3 us (12%)
  blocking collectives  11.1 us (9%)
  matrix products  8.62 us (7%)
    all_to_all x1, starting transfers between devices, on_device(): lax.all_to_all(coefficients, 'shard', split_axis=1, concat_axis=2, tiled=...  18.3 us
    all_to_all x1, starting transfers between devices, on_device(): lax.all_to_all(spectra, 'shard', split_axis=0, concat_axis=3, tiled=True)  14 us
    all_to_all x1, waiting for transfers between devices, on_device(): lax.all_to_all(spectra, 'shard', split_axis=0, concat_axis=3, tiled=True)  13.5 us
    cos x1, other arithmetic, longitude_tables(): jnp.cos(inner_angle)  11.4 us
    unnamed x1, blocking collectives  11.1 us
    dot_general x1, matrix products, on_device(): jnp.dot(left_side, lon_table, precision=lax.Precision.HIGHEST, preferred_...  5.9 us
    unnamed x11, local copies, waits for them, and re-layouts  5.07 us
    all_to_all x1, local copies, waits for them, and re-layouts, on_device(): lax.all_to_all(spectra, 'shard', split_axis=0, concat_axis=3, tiled=True)  3.06 us
  transfers between devices with their start and end apart: 3, of which 1 were waited for; matrix products, arithmetic and copies ran while one was open for 20% of the time, Pallas kernels for 0%

commit v1 on v0

v1 whole, which is shorter than its diff:
```python
import functools

import jax
import jax.numpy as jnp
from jax import lax
from jax.experimental import pallas as pl
from jax.experimental.pallas import tpu as pltpu
from jax.sharding import PartitionSpec as P

DEGS = 5120
NLON = 21600
PAIRS = 128
CYCLES = 512
SPAN = 40
LANES = 128
COLS = DEGS // LANES
HALF = COLS // 2
INNER = 256
OUTER = -(-NLON // INNER)
TURNS = 88
F32 = jnp.float32
BF16 = jnp.bfloat16
VMEM = pl.BlockSpec(memory_space=pltpu.VMEM)
HBM = pl.BlockSpec(memory_space=pltpu.HBM)


def params(mib):
    return pltpu.CompilerParams(vmem_limit_bytes=mib * 2**20)


def iota(shape, axis):
    return lax.broadcasted_iota(jnp.int32, shape, axis)


def send_kernel(coef_ref, out_ref, lines_ref, sems):
    shard = lax.axis_index("shard")
    lines_ref[...] = jnp.zeros_like(lines_ref)
    copies = []
    for k in range(2):
        for g in range(0, SPAN, 8):
            start = pl.multiple_of(lax.rem(shard * SPAN + (64 * k + g), LANES), 8)
            copies.append(
                pltpu.make_async_copy(
                    coef_ref.at[k, pl.ds(g, 8), :], lines_ref.at[pl.ds(start, 8), :], sems.at[k, g // 8]
                )
            )
            copies[-1].start()
    for copy in copies:
        copy.wait()
    out_ref[...] = lines_ref[...].T


def turn(phase):
    rest = wrap(phase)
    half = rest * (jnp.pi / NLON)
    square = half * half
    sine = jnp.full_like(half, -1.0 / 39916800.0)
    for c in (1.0 / 362880.0, -1.0 / 5040.0, 1.0 / 120.0, -1.0 / 6.0, 1.0):
        sine = sine * square + c
    sine = sine * half
    cosine = jnp.full_like(half, 1.0 / 479001600.0)
    for c in (-1.0 / 3628800.0, 1.0 / 40320.0, -1.0 / 720.0, 1.0 / 24.0, -0.5, 1.0):
        cosine = cosine * square + c
    return 1.0 - 2.0 * sine * sine, 2.0 * sine * cosine


def wrap(phase):
    return phase - jnp.round(phase * (1.0 / NLON)) * NLON


def table_kernel(orders_ref, lon_ref, turns_ref, cycles_ref):
    low = orders_ref[...].astype(F32)
    for j in range(2):
        order = low if j == 0 else DEGS - low
        inner = iota((INNER, PAIRS), 0).astype(F32)
        cosine, sine = turn(inner * order)
        lon_ref[:, pl.ds(j * PAIRS, PAIRS)] = cosine.astype(BF16)
        lon_ref[:, pl.ds((2 + j) * PAIRS, PAIRS)] = sine.astype(BF16)
        outer = iota((TURNS, PAIRS), 0).astype(F32)
        cosine, sine = turn(wrap(outer * order) * INNER)
        turns_ref[pl.ds(0, TURNS), pl.ds(j * PAIRS, PAIRS)] = cosine
        turns_ref[pl.ds(TURNS, TURNS), pl.ds(j * PAIRS, PAIRS)] = sine
    offset = (iota((8, CYCLES), 1).astype(F32) + (0.5 - CYCLES / 2)) * (jnp.pi / (2 * CYCLES))
    square = offset * offset
    sine = jnp.full_like(offset, 1.0 / 40320.0)
    for c in (-1.0 / 720.0, 1.0 / 24.0, -0.5, 1.0):
        sine = sine * square + c
    cosine = jnp.full_like(offset, 1.0 / 362880.0)
    for c in (-1.0 / 5040.0, 1.0 / 120.0, -1.0 / 6.0, 1.0):
        cosine = cosine * square + c
    row = iota((8, CYCLES), 0)
    own = jnp.sum(jnp.where(iota((1, PAIRS), 1) == lax.axis_index("shard"), low, 0.0), axis=1, keepdims=True)
    factor = jnp.where((row & 1) == 0, own, DEGS - own) / DEGS
    factor = jnp.where(row < 6, factor, -factor)
    cycles_ref[pl.ds(0, 8), :] = jnp.where(row < 4, -cosine * offset, factor) / sine
    cycles_ref[pl.ds(8, 8), :] = jnp.broadcast_to(own, (8, CYCLES))


def pack_kernel(cycles_ref, got_ref, weight_ref, flat_ref):
    group_zero = lax.axis_index("comp") == 0
    band = lax.axis_index("band")
    order = jnp.max(cycles_ref[8:16, 0:LANES]).astype(jnp.int32)
    lane = iota((8, LANES), 1)
    row = iota((8, LANES), 0)
    upper = row < 4
    columns = [None] * COLS
    on_cos = (row & 2) == 0
    for w in range(DEGS // SPAN // 4):
        four = got_ref[pl.ds(8 * w, 8), :]
        moved = pltpu.roll(four, 64, 1)
        turned = [(pltpu.roll(four, 2 * a, 0) if a else four) for a in range(4)]
        turned_sin = [(pltpu.roll(moved, 2 * a, 0) if a else moved) for a in range(4)]
        mixed = [jnp.where(on_cos, turned[a], turned_sin[(a + 1) % 4]) for a in range(4)]
        for t in range(4):
            piece = jnp.where(upper, mixed[-t % 4], mixed[(2 - t) % 4])
            first = SPAN * (4 * w + t)
            for v in range(first // LANES, (first + SPAN - 1) // LANES + 1):
                if columns[v] is None:
                    columns[v] = piece
                else:
                    columns[v] = jnp.where(lane >= first - LANES * v, piece, columns[v])
    for v in range(COLS):
        flat_ref[v] = columns[v]
    flat_ref[pl.ds(COLS, HALF)] = jnp.zeros((HALF, 8, LANES), F32)
    chunk = order // LANES
    rest = order - chunk * LANES
    back = lax.rem(LANES - rest, LANES)
    second_order = (row & 1) == 1
    for v in range(HALF):
        low = pltpu.roll(flat_ref[HALF * band + chunk + v], back, 1)
        high = pltpu.roll(flat_ref[jnp.minimum(HALF * band + chunk + v + 1, COLS + HALF - 1)], back, 1)
        lead = jnp.where(lane < LANES - rest, low, high)
        tail = flat_ref[HALF * band + v]
        position = (HALF * band + v) * LANES + lane
        inside = position < DEGS - order
        value = jnp.where(inside == second_order, 0.0, jnp.where(second_order, tail, lead))
        degree = jnp.where(inside, position + order, position).astype(F32)
        linear = (degree + 1.0) / DEGS
        shifted = (degree + 2.0) / DEGS
        on_values = jnp.where(group_zero, jnp.where(upper, linear * shifted, linear), jnp.where(upper, shifted, 0.0))
        on_deriv = jnp.where(upper, jnp.where(group_zero, 0.0, shifted), 1.0)
        both = jnp.concatenate([on_values * value, on_deriv * value], axis=0)
        weight_ref[:, pl.ds(v * LANES, LANES)] = both.astype(BF16)


def sums_kernel(cycles_ref, weight_ref, own_ref, deriv_ref, other_ref, out_ref, spec_ref, turned_ref):
    group_zero = lax.axis_index("comp") == 0
    weights = weight_ref[...]
    from_own = jnp.dot(weights, own_ref[...], preferred_element_type=F32)
    from_deriv = jnp.dot(weights, deriv_ref[...], preferred_element_type=F32)
    from_other = jnp.dot(weights, other_ref[...], preferred_element_type=F32)
    from_values = jnp.concatenate(
        [jnp.where(group_zero, from_own, from_other), jnp.where(group_zero, from_other, from_own)], axis=1
    )
    zero = from_values[0:4]
    one = from_values[4:8] + from_deriv[8:12]
    two = from_deriv[12:16]
    cotangent = cycles_ref[0:4]
    factor = cycles_ref[4:8]
    along = two - one

    def crossed(x):
        return factor * jnp.concatenate([x[2:4], x[0:2]], axis=0)

    parts = (
        jnp.where(group_zero, along, one + cotangent * zero),
        jnp.where(group_zero, -along - zero, crossed(zero)),
        jnp.where(group_zero, zero, crossed(two)),
    )
    spec_ref[...] = jnp.zeros_like(spec_ref)
    for c in range(3):
        for part in range(4):
            spec_ref[pl.ds(8 * part + 2 * c, 1), :] = parts[c][part : part + 1]
    turned_ref[...] = spec_ref[...].T
    for b in range(2):
        even = turned_ref[pl.ds(2 * b, PAIRS, stride=4), :]
        odd = turned_ref[pl.ds(2 * b + 1, PAIRS, stride=4), :]
        out_ref[pl.ds(b * PAIRS, PAIRS), :] = even + pltpu.roll(odd, 1, 1)


def field_kernel(got_ref, lon_ref, turns_ref, out_ref, left_ref):
    summed = got_ref[pl.ds(0, PAIRS), :] + got_ref[pl.ds(PAIRS, PAIRS), :]
    rows = summed.T
    cos_part = jnp.concatenate([rows[0:8], rows[8:16]], axis=1)
    sin_part = jnp.concatenate([rows[16:24], rows[24:32]], axis=1)
    for n in range(0, TURNS, 2):
        halves = []
        for d in range(2):
            turn_cos = turns_ref[pl.ds(n + d, 1), :]
            turn_sin = turns_ref[pl.ds(TURNS + n + d, 1), :]
            halves.append(
                jnp.concatenate(
                    [cos_part * turn_cos + sin_part * turn_sin, sin_part * turn_cos - cos_part * turn_sin], axis=1
                )
            )
        left_ref[pl.ds(8 * n, 16), :] = jnp.concatenate(halves, axis=0).astype(BF16)
    lon = lon_ref[...]
    step = 8
    for n in range(0, TURNS, step):
        field = lax.dot_general(
            left_ref[pl.ds(8 * n, 8 * step), :], lon, (((1,), (1,)), ((), ())), preferred_element_type=F32
        )
        for d in range(step):
            start = (n + d) * INNER
            width = min(INNER, NLON - start)
            if width <= 0:
                continue
            for c in range(3):
                out_ref[c, :, pl.ds(start, width)] = field[8 * d + 2 * c : 8 * d + 2 * c + 2, :width]


def on_device(coefficients, pair_orders, legendre, derivative):
    sent = pl.pallas_call(
        send_kernel,
        out_shape=jax.ShapeDtypeStruct((2 * PAIRS, LANES), F32),
        in_specs=[HBM],
        out_specs=VMEM,
        scratch_shapes=[pltpu.VMEM((LANES, 2 * PAIRS), F32), pltpu.SemaphoreType.DMA((2, SPAN // 8))],
        compiler_params=params(60),
        name="send",
    )(coefficients.transpose(0, 2, 1))
    sent, own = lax.optimization_barrier((sent, legendre[0]))
    got = lax.all_to_all(sent.reshape(PAIRS, 2, LANES), "shard", split_axis=0, concat_axis=0, tiled=True)
    other = lax.ppermute(own, "comp", [(0, 1), (1, 0)])
    lon, turns, cycles = pl.pallas_call(
        table_kernel,
        out_shape=(
            jax.ShapeDtypeStruct((INNER, 4 * PAIRS), BF16),
            jax.ShapeDtypeStruct((2 * TURNS, 2 * PAIRS), F32),
            jax.ShapeDtypeStruct((16, CYCLES), F32),
        ),
        in_specs=[VMEM],
        out_specs=(VMEM, VMEM, VMEM),
        compiler_params=params(4),
        cost_estimate=pl.CostEstimate(flops=400_000_000, bytes_accessed=600_000, transcendentals=0),
        name="tables",
    )(pair_orders.reshape(1, PAIRS))
    weights = pl.pallas_call(
        pack_kernel,
        out_shape=jax.ShapeDtypeStruct((16, HALF * LANES), BF16),
        in_specs=[VMEM, VMEM],
        out_specs=VMEM,
        scratch_shapes=[pltpu.VMEM((COLS + HALF, 8, LANES), F32)],
        compiler_params=params(4),
        cost_estimate=pl.CostEstimate(flops=30_000_000_000, bytes_accessed=300_000, transcendentals=0),
        name="pack",
    )(cycles, got.reshape(2 * PAIRS, LANES))
    spectra = pl.pallas_call(
        sums_kernel,
        out_shape=jax.ShapeDtypeStruct((2 * PAIRS, LANES), F32),
        in_specs=[VMEM] * 5,
        out_specs=VMEM,
        scratch_shapes=[pltpu.VMEM((LANES, CYCLES), F32), pltpu.VMEM((CYCLES, LANES), F32)],
        compiler_params=params(8),
        name="sums",
    )(cycles, weights, own, derivative[0, 0], other)
    pieces = lax.all_to_all(
        spectra.reshape(2 * PAIRS, 1, LANES), ("band", "shard"), split_axis=0, concat_axis=0, tiled=True
    )
    fields = pl.pallas_call(
        field_kernel,
        out_shape=jax.ShapeDtypeStruct((3, 2, NLON), F32),
        in_specs=[VMEM, VMEM, VMEM],
        out_specs=VMEM,
        scratch_shapes=[pltpu.VMEM((8 * TURNS, 4 * PAIRS), BF16)],
        compiler_params=params(8),
        name="fields",
    )(pieces.reshape(2 * PAIRS, LANES), lon, turns)
    return fields.transpose(1, 0, 2)


def solution(mesh):
    placed = (
        P(None, None, "shard"),
        P(),
        P("shard", "band", "comp"),
        P("comp", "shard", "band", None),
    )
    return jax.shard_map(
        on_device,
        mesh=mesh,
        in_specs=placed,
        out_specs=P(("shard", "band"), "comp", None),
        check_vma=False,
    )
```

time: 117 us -> 61 us (0.52)
  between operations: 17.6 us -> 0.06 us
  other arithmetic: 17 us -> 0 us
  local copies, waits for them, and re-layouts: 15.6 us -> 2.47 us
  starting transfers between devices: 32.3 us -> 20.2 us
  blocking collectives: 11.1 us -> 22.9 us
  matrix products: 8.62 us -> 0 us
  Pallas kernels: 0 us -> 5.35 us
  waiting for transfers between devices: 14.3 us -> 9.66 us
    all_to_all x0 -> x1, blocking collectives: none -> 22.9 us  [on_device(): lax.all_to_all(spectra.reshape(2 * PAIRS, 1, LANES), ('band', 'shard'), s...]
    all_to_all x2 -> x1, starting transfers between devices: 32.3 us -> 18.3 us  [on_device(): lax.all_to_all(sent.reshape(PAIRS, 2, LANES), 'shard', split_axis=0, conc...]
    cos x2 -> x0, other arithmetic: 11.5 us -> none  [the longest x1 11.4 us: longitude_tables(): jnp.cos(inner_angle)]
    unnamed x1 -> x0, blocking collectives: 11.1 us -> none
    dot_general x3 -> x0, matrix products: 8.62 us -> none  [the longest x1 5.9 us: on_device(): jnp.dot(left_side, lon_table, precision=lax.Precision.HIGHEST, preferred_...]
    pallas_call x0 -> x5, Pallas kernels: none -> 5.35 us  [the longest x1 1.8 us: on_device(): pl.pallas_call(field_kernel, out_shape=jax.ShapeDtypeStruct((3, 2, NLON),...]
    all_to_all x2 -> x1, waiting for transfers between devices: 13.5 us -> 9.66 us  [on_device(): lax.all_to_all(sent.reshape(PAIRS, 2, LANES), 'shard', split_axis=0, conc...]
    all_to_all x4 -> x0, local copies, waits for them, and re-layouts: 3.61 us -> none  [the longest x1 3.06 us: on_device(): lax.all_to_all(spectra, 'shard', split_axis=0, concat_axis=3, tiled=True)]
  transfers between devices with their start and end apart: 3 -> 2, of which waited for: 1 -> 1; matrix products, arithmetic and copies ran while one was open for 20% -> 0% of each run, Pallas kernels for 0% -> 1%
where the time goes in v1:
time: 61 us; the launch traced here: 60.7 us
  blocking collectives  22.9 us (38%)
  starting transfers between devices  20.2 us (33%)
  waiting for transfers between devices  9.66 us (16%)
  Pallas kernels  5.35 us (9%)
  local copies, waits for them, and re-layouts  2.47 us (4%)
    all_to_all x1, blocking collectives, on_device(): lax.all_to_all(spectra.reshape(2 * PAIRS, 1, LANES), ('band', 'shard'), s...  22.9 us
    all_to_all x1, starting transfers between devices, on_device(): lax.all_to_all(sent.reshape(PAIRS, 2, LANES), 'shard', split_axis=0, conc...  18.3 us
    all_to_all x1, waiting for transfers between devices, on_device(): lax.all_to_all(sent.reshape(PAIRS, 2, LANES), 'shard', split_axis=0, conc...  9.66 us
    unnamed x6, local copies, waits for them, and re-layouts  2.47 us
    ppermute x1, starting transfers between devices, on_device(): other = lax.ppermute(own, 'comp', [(0, 1), (1, 0)])  1.92 us
    pallas_call x1, Pallas kernels, on_device(): pl.pallas_call(field_kernel, out_shape=jax.ShapeDtypeStruct((3, 2, NLON),...  1.8 us
    pallas_call x1, Pallas kernels, on_device(): pl.pallas_call(send_kernel, out_shape=jax.ShapeDtypeStruct((2 * PAIRS, LA...  1.7 us
  transfers between devices with their start and end apart: 2, of which 1 were waited for; matrix products, arithmetic and copies ran while one was open for 0% of the time, Pallas kernels for 1%

profile of v1, /device:TPU:8, one launch (start us, length us, event | category | flops | bytes accessed | tf_op | source)
XLA Modules:
  0.0 60.7 jit_solution(9119715429471675034)
XLA Ops:
  0.0 1.7 %send.1 = f32[256,128]{1,0:T(8,128)} custom-call(f32[2,40,256]{2,1,0:T(8,128)} %bitcast.19), custom_call_target="tpu_custom_call" | custom-call | tf_op jit(solution)/shard_map/send/pallas_call | solution.py:213
  1.7 18.3 %all-to-all-start = ((f32[128,2,128]{2,1,0:T(2,128)}), f32[128,2,128]{2,1,0:T(2,128)S(1)}, u32[]{:S(2)}, u32[]{:S(2)}) async-start(f32[128,2,128]{2,1,0:T(2,128)} %bitcast.18), calls=%async_computation | async-start | bytes 262144 | tf_op jit(solution)/shard_map/all_to_all | solution.py:223
  20.0 1.9 %collective-permute-start = (bf16[2560,256]{1,0:T(8,128)(2,1)}, bf16[2560,256]{1,0:T(8,128)(2,1)S(1)}, u32[]{:S(2)}, u32[]{:S(2)}) collective-permute-start(bf16[2560,256]{1,0:T(8,128)(2,1)} %bitcast.12), channel_id=1, source_target_pairs={{0,2},{2,0},{1,3},{3,1},{4,6},{6,4},{5,7},{7,5},{8,10},{10,8},{9,1... | collective-permute-start | bytes 3932168 | tf_op jit(solution)/shard_map/ppermute | solution.py:224
  22.0 0.0 copy-start.2
  22.0 0.6 %copy-done.2 = s32[128]{0:T(128)S(1)} copy-done((s32[128]{0:T(128)S(1)}, s32[128]{0:T(128)}, u32[]{:S(2)}) %copy-start.2) | copy-done | bytes 536
  22.6 0.5 tables.1
  23.2 9.7 %all-to-all-done = f32[128,2,128]{2,1,0:T(2,128)S(1)} async-done(((f32[128,2,128]{2,1,0:T(2,128)}), f32[128,2,128]{2,1,0:T(2,128)S(1)}, u32[]{:S(2)}, u32[]{:S(2)}) %all-to-all-start) | async-done | bytes 131104 | tf_op jit(solution)/shard_map/all_to_all | solution.py:223
  32.8 0.0 copy-start
  32.8 0.0 copy-start.1
  32.8 0.3 pack.1.weight_ref
  33.1 0.0 collective-permute-done.other_ref
  33.1 1.5 %copy-done = bf16[1,1,2560,512]{3,2,1,0:T(8,128)(2,1)S(1)} copy-done((bf16[1,1,2560,512]{3,2,1,0:T(8,128)(2,1)S(1)}, bf16[1,1,2560,512]{3,2,1,0:T(8,128)(2,1)}, u32[]{:S(2)}) %copy-start) | copy-done | bytes 2621464
  34.6 0.4 copy-done.1
  34.9 1.0 %sums.1 = f32[256,128]{1,0:T(8,128)S(1)} custom-call(f32[16,512]{1,0:T(8,128)S(1)} %get-tuple-element.10.cycles_ref, bf16[16,2560]{1,0:T(8,128)(2,1)S(1)} %pack.1.weight_ref, bf16[2560,256]{1,0:T(8,128)(2,1)S(1)} %bitcast.13, bf16[2560,512]{1,0:T(8,128)(2,1)S(1)} %bitcast.11, bf16[2560,256]{1,0:T(8,128)(2,1)S(1)} %collective-permute-done.other_ref), custom_call_target="tpu_custom_call" | custom-call | tf_op jit(solution)/shard_map/sums/pallas_call | solution.py:248
  36.0 22.9 %all_to_all.10 = f32[256,1,128]{2,1,0:T(1,128)S(1)} all-to-all(f32[256,1,128]{2,1,0:T(1,128)S(1)} %bitcast.15), channel_id=1, replica_groups=mesh['shard'=128,'comp'=2,'band'=2] {'band','shard'}, dimensions={0} | all-to-all | bytes 262144 | tf_op jit(solution)/shard_map/all_to_all | solution.py:257
  58.9 1.8 %fields.1 = f32[3,2,21600]{2,1,0:T(2,128)} custom-call(f32[256,128]{1,0:T(8,128)S(1)} %bitcast.14, bf16[256,512]{1,0:T(8,128)(2,1)S(1)} %get-tuple-element.13.lon_ref, f32[176,256]{1,0:T(8,128)S(1)} %get-tuple-element.14.turns_ref), custom_call_target="tpu_custom_call" | custom-call | tf_op jit(solution)/shard_map/fields/pallas_call | solution.py:260
Async XLA Ops:
  1.7 31.1 %all-to-all-start = ((f32[128,2,128]{2,1,0:T(2,128)}), f32[128,2,128]{2,1,0:T(2,128)S(1)}, u32[]{:S(2)}, u32[]{:S(2)}) async-start(f32[128,2,128]{2,1,0:T(2,128)} %bitcast.18), calls=%async_computation | async-start | bytes 262144 | tf_op jit(solution)/shard_map/all_to_all | solution.py:223
  20.0 13.1 %collective-permute-start = (bf16[2560,256]{1,0:T(8,128)(2,1)}, bf16[2560,256]{1,0:T(8,128)(2,1)S(1)}, u32[]{:S(2)}, u32[]{:S(2)}) collective-permute-start(bf16[2560,256]{1,0:T(8,128)(2,1)} %bitcast.12), channel_id=1, source_target_pairs={{0,2},{2,0},{1,3},{3,1},{4,6},{6,4},{5,7},{7,5},{8,10},{10,8},{9,1... | collective-permute-start | bytes 3932168 | tf_op jit(solution)/shard_map/ppermute | solution.py:224
  22.0 0.7 %copy-start.2 = (s32[128]{0:T(128)S(1)}, s32[128]{0:T(128)}, u32[]{:S(2)}) copy-start(s32[128]{0:T(128)} %param.5) | copy-start | bytes 1540
  32.8 1.7 %copy-start = (bf16[1,1,2560,512]{3,2,1,0:T(8,128)(2,1)S(1)}, bf16[1,1,2560,512]{3,2,1,0:T(8,128)(2,1)}, u32[]{:S(2)}) copy-start(bf16[1,1,2560,512]{3,2,1,0:T(8,128)(2,1)} %param.7) | copy-start | bytes 7864324
  32.8 2.1 %copy-start.1 = (bf16[1,2560,256]{2,1,0:T(8,128)(2,1)S(1)}, bf16[1,2560,256]{2,1,0:T(8,128)(2,1)}, u32[]{:S(2)}) copy-start(bf16[1,2560,256]{2,1,0:T(8,128)(2,1)} %param.6) | copy-start | bytes 3932164

commit v2 on v1

--- a/solution.py
+++ b/solution.py
@@ -18,6 +18,7 @@
 INNER = 256
 OUTER = -(-NLON // INNER)
 TURNS = 88
+FIRST = 76
 F32 = jnp.float32
 BF16 = jnp.bfloat16
 VMEM = pl.BlockSpec(memory_space=pltpu.VMEM)
@@ -47,7 +48,9 @@
             copies[-1].start()
     for copy in copies:
         copy.wait()
-    out_ref[...] = lines_ref[...].T
+    rows = lines_ref[...].T
+    out_ref[pl.ds(0, 2 * (PAIRS - FIRST)), :] = rows[2 * FIRST :]
+    out_ref[pl.ds(2 * (PAIRS - FIRST), 2 * FIRST), :] = rows[: 2 * FIRST]
 
 
 def turn(phase):
@@ -106,7 +109,7 @@
     columns = [None] * COLS
     on_cos = (row & 2) == 0
     for w in range(DEGS // SPAN // 4):
-        four = got_ref[pl.ds(8 * w, 8), :]
+        four = got_ref[pl.ds(2 * ((4 * w - FIRST) % PAIRS), 8), :]
         moved = pltpu.roll(four, 64, 1)
         turned = [(pltpu.roll(four, 2 * a, 0) if a else four) for a in range(4)]
         turned_sin = [(pltpu.roll(moved, 2 * a, 0) if a else moved) for a in range(4)]
@@ -173,14 +176,15 @@
             spec_ref[pl.ds(8 * part + 2 * c, 1), :] = parts[c][part : part + 1]
     turned_ref[...] = spec_ref[...].T
     for b in range(2):
-        even = turned_ref[pl.ds(2 * b, PAIRS, stride=4), :]
-        odd = turned_ref[pl.ds(2 * b + 1, PAIRS, stride=4), :]
-        out_ref[pl.ds(b * PAIRS, PAIRS), :] = even + pltpu.roll(odd, 1, 1)
+        for first, count, place in ((FIRST, PAIRS - FIRST, 0), (0, FIRST, PAIRS - FIRST)):
+            even = turned_ref[pl.ds(4 * first + 2 * b, count, stride=4), :]
+            odd = turned_ref[pl.ds(4 * first + 2 * b + 1, count, stride=4), :]
+            out_ref[pl.ds(b * PAIRS + place, count), :] = even + pltpu.roll(odd, 1, 1)
 
 
 def field_kernel(got_ref, lon_ref, turns_ref, out_ref, left_ref):
     summed = got_ref[pl.ds(0, PAIRS), :] + got_ref[pl.ds(PAIRS, PAIRS), :]
-    rows = summed.T
+    rows = pltpu.roll(summed.T, FIRST, 1)
     cos_part = jnp.concatenate([rows[0:8], rows[8:16]], axis=1)
     sin_part = jnp.concatenate([rows[16:24], rows[24:32]], axis=1)
     for n in range(0, TURNS, 2):
@@ -220,7 +224,10 @@
         name="send",
     )(coefficients.transpose(0, 2, 1))
     sent, own = lax.optimization_barrier((sent, legendre[0]))
-    got = lax.all_to_all(sent.reshape(PAIRS, 2, LANES), "shard", split_axis=0, concat_axis=0, tiled=True)
+    shards = [(FIRST + i) % PAIRS for i in range(PAIRS)]
+    got = lax.all_to_all(
+        sent.reshape(PAIRS, 2, LANES), "shard", 0, 0, axis_index_groups=[shards], tiled=True
+    )
     other = lax.ppermute(own, "comp", [(0, 1), (1, 0)])
     lon, turns, cycles = pl.pallas_call(
         table_kernel,
@@ -255,7 +262,8 @@
         name="sums",
     )(cycles, weights, own, derivative[0, 0], other)
     pieces = lax.all_to_all(
-        spectra.reshape(2 * PAIRS, 1, LANES), ("band", "shard"), split_axis=0, concat_axis=0, tiled=True
+        spectra.reshape(2 * PAIRS, 1, LANES), ("band", "shard"), 0, 0,
+        axis_index_groups=[[PAIRS * b + s for b in range(2) for s in shards]], tiled=True,
     )
     fields = pl.pallas_call(
         field_kernel,

time: 61 us -> 54.6 us (0.90)
  the two profiles are of different devices: /device:TPU:8 before, /device:TPU:2 now
where the time goes in v2:
time: 54.6 us; the launch traced here: 54.3 us
  blocking collectives  22.9 us (42%)
  starting transfers between devices  22.7 us (42%)
  Pallas kernels  5.43 us (10%)
  waiting for transfers between devices  1.72 us (3%)
  local copies, waits for them, and re-layouts  1.45 us (3%)
    all_to_all x1, blocking collectives, on_device(): lax.all_to_all(spectra.reshape(2 * PAIRS, 1, LANES), ('band', 'shard'), 0...  22.9 us
    all_to_all x1, starting transfers between devices, on_device(): lax.all_to_all(sent.reshape(PAIRS, 2, LANES), 'shard', 0, 0, axis_index_g...  20.8 us
    ppermute x1, starting transfers between devices, on_device(): other = lax.ppermute(own, 'comp', [(0, 1), (1, 0)])  1.92 us
    pallas_call x1, Pallas kernels, on_device(): pl.pallas_call(field_kernel, out_shape=jax.ShapeDtypeStruct((3, 2, NLON),...  1.88 us
    pallas_call x1, Pallas kernels, on_device(): pl.pallas_call(send_kernel, out_shape=jax.ShapeDtypeStruct((2 * PAIRS, LA...  1.7 us
    unnamed x6, local copies, waits for them, and re-layouts  1.45 us
  transfers between devices with their start and end apart: 2, of which 2 were waited for; matrix products, arithmetic and copies ran while one was open for 0% of the time, Pallas kernels for 2%

profile of v2, /device:TPU:2, one launch (start us, length us, event | category | flops | bytes accessed | tf_op | source)
XLA Modules:
  0.0 54.3 jit_solution(10022140958174727656)
XLA Ops:
  0.0 1.7 %send.1 = f32[256,128]{1,0:T(8,128)} custom-call(f32[2,40,256]{2,1,0:T(8,128)} %bitcast.19), custom_call_target="tpu_custom_call" | custom-call | tf_op jit(solution)/shard_map/send/pallas_call | solution.py:217
  1.7 20.8 %all-to-all-start = ((f32[128,2,128]{2,1,0:T(2,128)}), f32[128,2,128]{2,1,0:T(2,128)S(1)}, u32[]{:S(2)}, u32[]{:S(2)}) async-start(f32[128,2,128]{2,1,0:T(2,128)} %bitcast.18), calls=%async_computation | async-start | bytes 262144 | tf_op jit(solution)/shard_map/all_to_all | solution.py:228
  22.5 1.9 %collective-permute-start = (bf16[2560,256]{1,0:T(8,128)(2,1)}, bf16[2560,256]{1,0:T(8,128)(2,1)S(1)}, u32[]{:S(2)}, u32[]{:S(2)}) collective-permute-start(bf16[2560,256]{1,0:T(8,128)(2,1)} %bitcast.12), channel_id=1, source_target_pairs={{0,2},{2,0},{1,3},{3,1},{4,6},{6,4},{5,7},{7,5},{8,10},{10,8},{9,1... | collective-permute-start | bytes 3932168 | tf_op jit(solution)/shard_map/ppermute | solution.py:231
  24.5 0.0 copy-start.2
  24.5 0.6 %copy-done.2 = s32[128]{0:T(128)S(1)} copy-done((s32[128]{0:T(128)S(1)}, s32[128]{0:T(128)}, u32[]{:S(2)}) %copy-start.2) | copy-done | bytes 536
  25.1 0.5 %tables.1 = (bf16[256,512]{1,0:T(8,128)(2,1)S(1)}, f32[176,256]{1,0:T(8,128)S(1)}, f32[16,512]{1,0:T(8,128)S(1)}) custom-call(s32[1,128]{1,0:T(1,128)S(1)} %bitcast.17), custom_call_target="tpu_custom_call" | custom-call | flops 400000000 | bytes 600000 | tf_op jit(solution)/shard_map/tables/pallas_call | solution.py:232
  25.7 0.7 %all-to-all-done = f32[128,2,128]{2,1,0:T(2,128)S(1)} async-done(((f32[128,2,128]{2,1,0:T(2,128)}), f32[128,2,128]{2,1,0:T(2,128)S(1)}, u32[]{:S(2)}, u32[]{:S(2)}) %all-to-all-start) | async-done | bytes 131104 | tf_op jit(solution)/shard_map/all_to_all | solution.py:228
  26.4 0.0 copy-start
  26.4 0.0 copy-start.1
  26.4 0.3 pack.1.weight_ref
  26.6 1.0 %collective-permute-done.other_ref = bf16[2560,256]{1,0:T(8,128)(2,1)S(1)} collective-permute-done((bf16[2560,256]{1,0:T(8,128)(2,1)}, bf16[2560,256]{1,0:T(8,128)(2,1)S(1)}, u32[]{:S(2)}, u32[]{:S(2)}) %collective-permute-start) | collective-permute-done | bytes 1310752 | tf_op jit(solution)/shard_map/ppermute | solution.py:231
  27.7 0.4 copy-done
  28.1 0.4 copy-done.1
  28.5 1.0 %sums.1 = f32[256,128]{1,0:T(8,128)S(1)} custom-call(f32[16,512]{1,0:T(8,128)S(1)} %get-tuple-element.10.cycles_ref, bf16[16,2560]{1,0:T(8,128)(2,1)S(1)} %pack.1.weight_ref, bf16[2560,256]{1,0:T(8,128)(2,1)S(1)} %bitcast.13, bf16[2560,512]{1,0:T(8,128)(2,1)S(1)} %bitcast.11, bf16[2560,256]{1,0:T(8,128)(2,1)S(1)} %collective-permute-done.other_ref), custom_call_target="tpu_custom_call" | custom-call | tf_op jit(solution)/shard_map/sums/pallas_call | solution.py:255
  29.5 22.9 %all_to_all.10 = f32[256,1,128]{2,1,0:T(1,128)S(1)} all-to-all(f32[256,1,128]{2,1,0:T(1,128)S(1)} %bitcast.15), channel_id=1, replica_groups={{304,308,312,316,320,324,328,332,336,340,344,348,352,356,360,364,368,37..., dimensions={0} | all-to-all | bytes 262144 | tf_op jit(solution)/shard_map/all_to_all | solution.py:264
  52.4 1.9 %fields.1 = f32[3,2,21600]{2,1,0:T(2,128)} custom-call(f32[256,128]{1,0:T(8,128)S(1)} %bitcast.14, bf16[256,512]{1,0:T(8,128)(2,1)S(1)} %get-tuple-element.13.lon_ref, f32[176,256]{1,0:T(8,128)S(1)} %get-tuple-element.14.turns_ref), custom_call_target="tpu_custom_call" | custom-call | tf_op jit(solution)/shard_map/fields/pallas_call | solution.py:268
Async XLA Ops:
  1.7 24.7 %all-to-all-start = ((f32[128,2,128]{2,1,0:T(2,128)}), f32[128,2,128]{2,1,0:T(2,128)S(1)}, u32[]{:S(2)}, u32[]{:S(2)}) async-start(f32[128,2,128]{2,1,0:T(2,128)} %bitcast.18), calls=%async_computation | async-start | bytes 262144 | tf_op jit(solution)/shard_map/all_to_all | solution.py:228
  22.5 5.1 %collective-permute-start = (bf16[2560,256]{1,0:T(8,128)(2,1)}, bf16[2560,256]{1,0:T(8,128)(2,1)S(1)}, u32[]{:S(2)}, u32[]{:S(2)}) collective-permute-start(bf16[2560,256]{1,0:T(8,128)(2,1)} %bitcast.12), channel_id=1, source_target_pairs={{0,2},{2,0},{1,3},{3,1},{4,6},{6,4},{5,7},{7,5},{8,10},{10,8},{9,1... | collective-permute-start | bytes 3932168 | tf_op jit(solution)/shard_map/ppermute | solution.py:231
  24.5 0.7 %copy-start.2 = (s32[128]{0:T(128)S(1)}, s32[128]{0:T(128)}, u32[]{:S(2)}) copy-start(s32[128]{0:T(128)} %param.5) | copy-start | bytes 1540
  26.4 1.7 %copy-start = (bf16[1,1,2560,512]{3,2,1,0:T(8,128)(2,1)S(1)}, bf16[1,1,2560,512]{3,2,1,0:T(8,128)(2,1)}, u32[]{:S(2)}) copy-start(bf16[1,1,2560,512]{3,2,1,0:T(8,128)(2,1)} %param.7) | copy-start | bytes 7864324
  26.4 2.1 %copy-start.1 = (bf16[1,2560,256]{2,1,0:T(8,128)(2,1)S(1)}, bf16[1,2560,256]{2,1,0:T(8,128)(2,1)}, u32[]{:S(2)}) copy-start(bf16[1,2560,256]{2,1,0:T(8,128)(2,1)} %param.6) | copy-start | bytes 3932164

commit v3 on v2

--- a/solution.py
+++ b/solution.py
@@ -18,6 +18,7 @@
 INNER = 256
 OUTER = -(-NLON // INNER)
 TURNS = 88
+STEP = 22
 FIRST = 76
 F32 = jnp.float32
 BF16 = jnp.bfloat16
@@ -182,35 +183,41 @@
             out_ref[pl.ds(b * PAIRS + place, count), :] = even + pltpu.roll(odd, 1, 1)
 
 
-def field_kernel(got_ref, lon_ref, turns_ref, out_ref, left_ref):
+def field_kernel(got_ref, lon_ref, turns_ref, out_ref, left_ref, *rest):
+    parts, sems = rest[:-1], rest[-1]
     summed = got_ref[pl.ds(0, PAIRS), :] + got_ref[pl.ds(PAIRS, PAIRS), :]
     rows = pltpu.roll(summed.T, FIRST, 1)
     cos_part = jnp.concatenate([rows[0:8], rows[8:16]], axis=1)
     sin_part = jnp.concatenate([rows[16:24], rows[24:32]], axis=1)
-    for n in range(0, TURNS, 2):
-        halves = []
-        for d in range(2):
-            turn_cos = turns_ref[pl.ds(n + d, 1), :]
-            turn_sin = turns_ref[pl.ds(TURNS + n + d, 1), :]
-            halves.append(
-                jnp.concatenate(
-                    [cos_part * turn_cos + sin_part * turn_sin, sin_part * turn_cos - cos_part * turn_sin], axis=1
+    lon = lon_ref[...]
+    copies = []
+    for i, part_ref in enumerate(parts):
+        first = STEP * i
+        for n in range(first, first + STEP, 2):
+            halves = []
+            for d in range(2):
+                turn_cos = turns_ref[pl.ds(n + d, 1), :]
+                turn_sin = turns_ref[pl.ds(TURNS + n + d, 1), :]
+                halves.append(
+                    jnp.concatenate(
+                        [cos_part * turn_cos + sin_part * turn_sin, sin_part * turn_cos - cos_part * turn_sin], axis=1
+                    )
                 )
-            )
-        left_ref[pl.ds(8 * n, 16), :] = jnp.concatenate(halves, axis=0).astype(BF16)
-    lon = lon_ref[...]
-    step = 8
-    for n in range(0, TURNS, step):
+            left_ref[pl.ds(8 * n, 16), :] = jnp.concatenate(halves, axis=0).astype(BF16)
         field = lax.dot_general(
-            left_ref[pl.ds(8 * n, 8 * step), :], lon, (((1,), (1,)), ((), ())), preferred_element_type=F32
+            left_ref[pl.ds(8 * first, 8 * STEP), :], lon, (((1,), (1,)), ((), ())), preferred_element_type=F32
         )
-        for d in range(step):
-            start = (n + d) * INNER
-            width = min(INNER, NLON - start)
+        for d in range(STEP):
+            width = min(INNER, NLON - (first + d) * INNER)
             if width <= 0:
                 continue
             for c in range(3):
-                out_ref[c, :, pl.ds(start, width)] = field[8 * d + 2 * c : 8 * d + 2 * c + 2, :width]
+                part_ref[c, :, pl.ds(d * INNER, width)] = field[8 * d + 2 * c : 8 * d + 2 * c + 2, :width]
+        width = part_ref.shape[2]
+        copies.append(pltpu.make_async_copy(part_ref, out_ref.at[:, :, pl.ds(first * INNER, width)], sems.at[i]))
+        copies[-1].start()
+    for copy in copies:
+        copy.wait()
 
 
 def on_device(coefficients, pair_orders, legendre, derivative):
@@ -269,8 +276,12 @@
         field_kernel,
         out_shape=jax.ShapeDtypeStruct((3, 2, NLON), F32),
         in_specs=[VMEM, VMEM, VMEM],
-        out_specs=VMEM,
-        scratch_shapes=[pltpu.VMEM((8 * TURNS, 4 * PAIRS), BF16)],
+        out_specs=HBM,
+        scratch_shapes=[
+            pltpu.VMEM((8 * TURNS, 4 * PAIRS), BF16),
+            *[pltpu.VMEM((3, 2, min(STEP * INNER, NLON - n * INNER)), F32) for n in range(0, TURNS, STEP)],
+            pltpu.SemaphoreType.DMA((TURNS // STEP,)),
+        ],
         compiler_params=params(8),
         name="fields",
     )(pieces.reshape(2 * PAIRS, LANES), lon, turns)

time: 54.6 us -> 54.1 us (level)
  Pallas kernels: 5.43 us -> 4.88 us
where the time goes in v3:
time: 54.1 us; the launch traced here: 53.7 us
  blocking collectives  22.9 us (42%)
  starting transfers between devices  22.7 us (42%)
  Pallas kernels  4.88 us (9%)
  waiting for transfers between devices  1.72 us (3%)
  local copies, waits for them, and re-layouts  1.45 us (3%)
    all_to_all x1, blocking collectives, on_device(): lax.all_to_all(spectra.reshape(2 * PAIRS, 1, LANES), ('band', 'shard'), 0...  22.9 us
    all_to_all x1, starting transfers between devices, on_device(): lax.all_to_all(sent.reshape(PAIRS, 2, LANES), 'shard', 0, 0, axis_index_g...  20.8 us
    ppermute x1, starting transfers between devices, on_device(): other = lax.ppermute(own, 'comp', [(0, 1), (1, 0)])  1.92 us
    pallas_call x1, Pallas kernels, on_device(): pl.pallas_call(send_kernel, out_shape=jax.ShapeDtypeStruct((2 * PAIRS, LA...  1.7 us
    unnamed x6, local copies, waits for them, and re-layouts  1.45 us
    pallas_call x1, Pallas kernels, on_device(): pl.pallas_call(field_kernel, out_shape=jax.ShapeDtypeStruct((3, 2, NLON),...  1.33 us
  transfers between devices with their start and end apart: 2, of which 2 were waited for; matrix products, arithmetic and copies ran while one was open for 0% of the time, Pallas kernels for 2%

profile of v3, /device:TPU:2, one launch (start us, length us, event | category | flops | bytes accessed | tf_op | source)
XLA Modules:
  0.0 53.7 jit_solution(17568392109848809275)
XLA Ops:
  0.0 1.7 %send.1 = f32[256,128]{1,0:T(8,128)} custom-call(f32[2,40,256]{2,1,0:T(8,128)} %bitcast.19), custom_call_target="tpu_custom_call" | custom-call | tf_op jit(solution)/shard_map/send/pallas_call | solution.py:224
  1.7 20.8 %all-to-all-start = ((f32[128,2,128]{2,1,0:T(2,128)}), f32[128,2,128]{2,1,0:T(2,128)S(1)}, u32[]{:S(2)}, u32[]{:S(2)}) async-start(f32[128,2,128]{2,1,0:T(2,128)} %bitcast.18), calls=%async_computation | async-start | bytes 262144 | tf_op jit(solution)/shard_map/all_to_all | solution.py:235
  22.5 1.9 %collective-permute-start = (bf16[2560,256]{1,0:T(8,128)(2,1)}, bf16[2560,256]{1,0:T(8,128)(2,1)S(1)}, u32[]{:S(2)}, u32[]{:S(2)}) collective-permute-start(bf16[2560,256]{1,0:T(8,128)(2,1)} %bitcast.12), channel_id=1, source_target_pairs={{0,2},{2,0},{1,3},{3,1},{4,6},{6,4},{5,7},{7,5},{8,10},{10,8},{9,1... | collective-permute-start | bytes 3932168 | tf_op jit(solution)/shard_map/ppermute | solution.py:238
  24.5 0.0 copy-start.2
  24.5 0.6 %copy-done.2 = s32[128]{0:T(128)S(1)} copy-done((s32[128]{0:T(128)S(1)}, s32[128]{0:T(128)}, u32[]{:S(2)}) %copy-start.2) | copy-done | bytes 536
  25.1 0.5 %tables.1 = (bf16[256,512]{1,0:T(8,128)(2,1)S(1)}, f32[176,256]{1,0:T(8,128)S(1)}, f32[16,512]{1,0:T(8,128)S(1)}) custom-call(s32[1,128]{1,0:T(1,128)S(1)} %bitcast.17), custom_call_target="tpu_custom_call" | custom-call | flops 400000000 | bytes 600000 | tf_op jit(solution)/shard_map/tables/pallas_call | solution.py:239
  25.7 0.7 %all-to-all-done = f32[128,2,128]{2,1,0:T(2,128)S(1)} async-done(((f32[128,2,128]{2,1,0:T(2,128)}), f32[128,2,128]{2,1,0:T(2,128)S(1)}, u32[]{:S(2)}, u32[]{:S(2)}) %all-to-all-start) | async-done | bytes 131104 | tf_op jit(solution)/shard_map/all_to_all | solution.py:235
  26.4 0.0 copy-start
  26.4 0.0 copy-start.1
  26.4 0.3 pack.1.weight_ref
  26.6 1.0 %collective-permute-done.other_ref = bf16[2560,256]{1,0:T(8,128)(2,1)S(1)} collective-permute-done((bf16[2560,256]{1,0:T(8,128)(2,1)}, bf16[2560,256]{1,0:T(8,128)(2,1)S(1)}, u32[]{:S(2)}, u32[]{:S(2)}) %collective-permute-start) | collective-permute-done | bytes 1310752 | tf_op jit(solution)/shard_map/ppermute | solution.py:238
  27.7 0.4 copy-done
  28.1 0.4 copy-done.1
  28.5 1.0 %sums.1 = f32[256,128]{1,0:T(8,128)S(1)} custom-call(f32[16,512]{1,0:T(8,128)S(1)} %get-tuple-element.10.cycles_ref, bf16[16,2560]{1,0:T(8,128)(2,1)S(1)} %pack.1.weight_ref, bf16[2560,256]{1,0:T(8,128)(2,1)S(1)} %bitcast.13, bf16[2560,512]{1,0:T(8,128)(2,1)S(1)} %bitcast.11, bf16[2560,256]{1,0:T(8,128)(2,1)S(1)} %collective-permute-done.other_ref), custom_call_target="tpu_custom_call" | custom-call | tf_op jit(solution)/shard_map/sums/pallas_call | solution.py:262
  29.5 22.9 %all_to_all.10 = f32[256,1,128]{2,1,0:T(1,128)S(1)} all-to-all(f32[256,1,128]{2,1,0:T(1,128)S(1)} %bitcast.15), channel_id=1, replica_groups={{304,308,312,316,320,324,328,332,336,340,344,348,352,356,360,364,368,37..., dimensions={0} | all-to-all | bytes 262144 | tf_op jit(solution)/shard_map/all_to_all | solution.py:271
  52.4 1.3 %fields.1 = f32[3,2,21600]{2,1,0:T(2,128)} custom-call(f32[256,128]{1,0:T(8,128)S(1)} %bitcast.14, bf16[256,512]{1,0:T(8,128)(2,1)S(1)} %get-tuple-element.13.lon_ref, f32[176,256]{1,0:T(8,128)S(1)} %get-tuple-element.14.turns_ref), custom_call_target="tpu_custom_call" | custom-call | tf_op jit(solution)/shard_map/fields/pallas_call | solution.py:275
Async XLA Ops:
  1.7 24.7 %all-to-all-start = ((f32[128,2,128]{2,1,0:T(2,128)}), f32[128,2,128]{2,1,0:T(2,128)S(1)}, u32[]{:S(2)}, u32[]{:S(2)}) async-start(f32[128,2,128]{2,1,0:T(2,128)} %bitcast.18), calls=%async_computation | async-start | bytes 262144 | tf_op jit(solution)/shard_map/all_to_all | solution.py:235
  22.5 5.1 %collective-permute-start = (bf16[2560,256]{1,0:T(8,128)(2,1)}, bf16[2560,256]{1,0:T(8,128)(2,1)S(1)}, u32[]{:S(2)}, u32[]{:S(2)}) collective-permute-start(bf16[2560,256]{1,0:T(8,128)(2,1)} %bitcast.12), channel_id=1, source_target_pairs={{0,2},{2,0},{1,3},{3,1},{4,6},{6,4},{5,7},{7,5},{8,10},{10,8},{9,1... | collective-permute-start | bytes 3932168 | tf_op jit(solution)/shard_map/ppermute | solution.py:238
  24.5 0.7 %copy-start.2 = (s32[128]{0:T(128)S(1)}, s32[128]{0:T(128)}, u32[]{:S(2)}) copy-start(s32[128]{0:T(128)} %param.5) | copy-start | bytes 1540
  26.4 1.7 %copy-start = (bf16[1,1,2560,512]{3,2,1,0:T(8,128)(2,1)S(1)}, bf16[1,1,2560,512]{3,2,1,0:T(8,128)(2,1)}, u32[]{:S(2)}) copy-start(bf16[1,1,2560,512]{3,2,1,0:T(8,128)(2,1)} %param.7) | copy-start | bytes 7864324
  26.4 2.1 %copy-start.1 = (bf16[1,2560,256]{2,1,0:T(8,128)(2,1)S(1)}, bf16[1,2560,256]{2,1,0:T(8,128)(2,1)}, u32[]{:S(2)}) copy-start(bf16[1,2560,256]{2,1,0:T(8,128)(2,1)} %param.6) | copy-start | bytes 3932164

commit v4 on v3

--- a/solution.py
+++ b/solution.py
@@ -18,6 +18,8 @@
 INNER = 256
 OUTER = -(-NLON // INNER)
 TURNS = 88
+PARTS = 5
+PART = HALF * LANES // PARTS
 STEP = 22
 FIRST = 76
 F32 = jnp.float32
@@ -100,7 +102,18 @@
     cycles_ref[pl.ds(8, 8), :] = jnp.broadcast_to(own, (8, CYCLES))
 
 
-def pack_kernel(cycles_ref, got_ref, weight_ref, flat_ref):
+def pack_kernel(cycles_ref, got_ref, own_any, deriv_any, weight_ref, near_ref, flat_ref, own_ref, deriv_ref, sems):
+    copies = []
+    for c in range(PARTS):
+        rows = pl.ds(c * PART, PART)
+        copies.append(
+            (
+                pltpu.make_async_copy(own_any.at[rows, :], own_ref.at[rows, :], sems.at[0, c]),
+                pltpu.make_async_copy(deriv_any.at[rows, :], deriv_ref.at[rows, :], sems.at[1, c]),
+            )
+        )
+        for copy in copies[-1]:
+            copy.start()
     group_zero = lax.axis_index("comp") == 0
     band = lax.axis_index("band")
     order = jnp.max(cycles_ref[8:16, 0:LANES]).astype(jnp.int32)
@@ -145,14 +158,24 @@
         on_deriv = jnp.where(upper, jnp.where(group_zero, 0.0, shifted), 1.0)
         both = jnp.concatenate([on_values * value, on_deriv * value], axis=0)
         weight_ref[:, pl.ds(v * LANES, LANES)] = both.astype(BF16)
-
-
-def sums_kernel(cycles_ref, weight_ref, own_ref, deriv_ref, other_ref, out_ref, spec_ref, turned_ref):
+    from_own = jnp.zeros((16, CYCLES // 2), F32)
+    from_deriv = jnp.zeros((16, CYCLES), F32)
+    for c in range(PARTS):
+        for copy in copies[c]:
+            copy.wait()
+        rows = pl.ds(c * PART, PART)
+        weights = weight_ref[:, rows]
+        from_own += jnp.dot(weights, own_ref[rows, :], preferred_element_type=F32)
+        from_deriv += jnp.dot(weights, deriv_ref[rows, :], preferred_element_type=F32)
+    near_ref[:, pl.ds(0, CYCLES // 2)] = from_own
+    near_ref[:, pl.ds(CYCLES // 2, CYCLES)] = from_deriv
+
+
+def sums_kernel(cycles_ref, weight_ref, near_ref, other_ref, out_ref, spec_ref, turned_ref):
     group_zero = lax.axis_index("comp") == 0
-    weights = weight_ref[...]
-    from_own = jnp.dot(weights, own_ref[...], preferred_element_type=F32)
-    from_deriv = jnp.dot(weights, deriv_ref[...], preferred_element_type=F32)
-    from_other = jnp.dot(weights, other_ref[...], preferred_element_type=F32)
+    from_own = near_ref[:, : CYCLES // 2]
+    from_deriv = near_ref[:, CYCLES // 2 :]
+    from_other = jnp.dot(weight_ref[...], other_ref[...], preferred_element_type=F32)
     from_values = jnp.concatenate(
         [jnp.where(group_zero, from_own, from_other), jnp.where(group_zero, from_other, from_own)], axis=1
     )
@@ -249,25 +272,33 @@
         cost_estimate=pl.CostEstimate(flops=400_000_000, bytes_accessed=600_000, transcendentals=0),
         name="tables",
     )(pair_orders.reshape(1, PAIRS))
-    weights = pl.pallas_call(
+    weights, near = pl.pallas_call(
         pack_kernel,
-        out_shape=jax.ShapeDtypeStruct((16, HALF * LANES), BF16),
-        in_specs=[VMEM, VMEM],
-        out_specs=VMEM,
-        scratch_shapes=[pltpu.VMEM((COLS + HALF, 8, LANES), F32)],
-        compiler_params=params(4),
-        cost_estimate=pl.CostEstimate(flops=30_000_000_000, bytes_accessed=300_000, transcendentals=0),
+        out_shape=(
+            jax.ShapeDtypeStruct((16, HALF * LANES), BF16),
+            jax.ShapeDtypeStruct((16, CYCLES // 2 + CYCLES), F32),
+        ),
+        in_specs=[VMEM, VMEM, HBM, HBM],
+        out_specs=(VMEM, VMEM),
+        scratch_shapes=[
+            pltpu.VMEM((COLS + HALF, 8, LANES), F32),
+            pltpu.VMEM((HALF * LANES, CYCLES // 2), BF16),
+            pltpu.VMEM((HALF * LANES, CYCLES), BF16),
+            pltpu.SemaphoreType.DMA((2, PARTS)),
+        ],
+        compiler_params=params(52),
+        cost_estimate=pl.CostEstimate(flops=30_000_000_000, bytes_accessed=4_000_000, transcendentals=0),
         name="pack",
-    )(cycles, got.reshape(2 * PAIRS, LANES))
+    )(cycles, got.reshape(2 * PAIRS, LANES), own, derivative[0, 0])
     spectra = pl.pallas_call(
         sums_kernel,
         out_shape=jax.ShapeDtypeStruct((2 * PAIRS, LANES), F32),
-        in_specs=[VMEM] * 5,
+        in_specs=[VMEM] * 4,
         out_specs=VMEM,
         scratch_shapes=[pltpu.VMEM((LANES, CYCLES), F32), pltpu.VMEM((CYCLES, LANES), F32)],
         compiler_params=params(8),
         name="sums",
-    )(cycles, weights, own, derivative[0, 0], other)
+    )(cycles, weights, near, other)
     pieces = lax.all_to_all(
         spectra.reshape(2 * PAIRS, 1, LANES), ("band", "shard"), 0, 0,
         axis_index_groups=[[PAIRS * b + s for b in range(2) for s in shards]], tiled=True,

time: 54.1 us -> 53.8 us (level)
  Pallas kernels: 4.88 us -> 6.45 us
  waiting for transfers between devices: 1.72 us -> 0.7 us
  local copies, waits for them, and re-layouts: 1.45 us -> 0.65 us
    pallas_call x1, Pallas kernels: 0.27 us -> 2.26 us  [on_device(): pl.pallas_call(pack_kernel, out_shape=(jax.ShapeDtypeStruct((16, HALF * L...]
    ppermute x1, waiting for transfers between devices: 1.03 us -> 0.01 us  [on_device(): other = lax.ppermute(own, 'comp', [(0, 1), (1, 0)])]
    unnamed x6 -> x4, local copies, waits for them, and re-layouts: 1.45 us -> 0.65 us
  transfers between devices with their start and end apart: 2 -> 2, of which waited for: 2 -> 1; matrix products, arithmetic and copies ran while one was open for 0% -> 0% of each run, Pallas kernels for 2% -> 5%
where the time goes in v4:
time: 53.8 us; the launch traced here: 53.5 us
  blocking collectives  22.9 us (43%)
  starting transfers between devices  22.7 us (42%)
  Pallas kernels  6.45 us (12%)
  waiting for transfers between devices  0.7 us (1%)
  local copies, waits for them, and re-layouts  0.65 us (1%)
    all_to_all x1, blocking collectives, on_device(): lax.all_to_all(spectra.reshape(2 * PAIRS, 1, LANES), ('band', 'shard'), 0...  22.9 us
    all_to_all x1, starting transfers between devices, on_device(): lax.all_to_all(sent.reshape(PAIRS, 2, LANES), 'shard', 0, 0, axis_index_g...  20.8 us
    pallas_call x1, Pallas kernels, on_device(): pl.pallas_call(pack_kernel, out_shape=(jax.ShapeDtypeStruct((16, HALF * L...  2.26 us
    ppermute x1, starting transfers between devices, on_device(): other = lax.ppermute(own, 'comp', [(0, 1), (1, 0)])  1.92 us
    pallas_call x1, Pallas kernels, on_device(): pl.pallas_call(send_kernel, out_shape=jax.ShapeDtypeStruct((2 * PAIRS, LA...  1.77 us
    pallas_call x1, Pallas kernels, on_device(): pl.pallas_call(field_kernel, out_shape=jax.ShapeDtypeStruct((3, 2, NLON),...  1.34 us
  transfers between devices with their start and end apart: 2, of which 1 were waited for; matrix products, arithmetic and copies ran while one was open for 0% of the time, Pallas kernels for 5%

profile of v4, /device:TPU:2, one launch (start us, length us, event | category | flops | bytes accessed | tf_op | source)
XLA Modules:
  0.0 53.5 jit_solution(16125826701678916741)
XLA Ops:
  0.0 0.0 copy-start
  0.0 1.8 %send.1 = f32[256,128]{1,0:T(8,128)} custom-call(f32[2,40,256]{2,1,0:T(8,128)} %bitcast.18), custom_call_target="tpu_custom_call" | custom-call | tf_op jit(solution)/shard_map/send/pallas_call | solution.py:247
  1.8 20.8 %all-to-all-start = ((f32[128,2,128]{2,1,0:T(2,128)}), f32[128,2,128]{2,1,0:T(2,128)S(1)}, u32[]{:S(2)}, u32[]{:S(2)}) async-start(f32[128,2,128]{2,1,0:T(2,128)} %bitcast.17), calls=%async_computation | async-start | bytes 262144 | tf_op jit(solution)/shard_map/all_to_all | solution.py:258
  22.6 1.9 %collective-permute-start = (bf16[2560,256]{1,0:T(8,128)(2,1)}, bf16[2560,256]{1,0:T(8,128)(2,1)S(1)}, u32[]{:S(2)}, u32[]{:S(2)}) collective-permute-start(bf16[2560,256]{1,0:T(8,128)(2,1)} %bitcast.14), channel_id=1, source_target_pairs={{0,2},{2,0},{1,3},{3,1},{4,6},{6,4},{5,7},{7,5},{8,10},{10,8},{9,1... | collective-permute-start | bytes 3932168 | tf_op jit(solution)/shard_map/ppermute | solution.py:261
  24.5 0.0 copy-start.1
  24.6 0.6 %copy-done.1 = s32[128]{0:T(128)S(1)} copy-done((s32[128]{0:T(128)S(1)}, s32[128]{0:T(128)}, u32[]{:S(2)}) %copy-start.1) | copy-done | bytes 536
  25.2 0.5 %tables.1 = (bf16[256,512]{1,0:T(8,128)(2,1)S(1)}, f32[176,256]{1,0:T(8,128)S(1)}, f32[16,512]{1,0:T(8,128)S(1)}) custom-call(s32[1,128]{1,0:T(1,128)S(1)} %bitcast.16), custom_call_target="tpu_custom_call" | custom-call | flops 400000000 | bytes 600000 | tf_op jit(solution)/shard_map/tables/pallas_call | solution.py:262
  25.7 0.7 %all-to-all-done = f32[128,2,128]{2,1,0:T(2,128)S(1)} async-done(((f32[128,2,128]{2,1,0:T(2,128)}), f32[128,2,128]{2,1,0:T(2,128)S(1)}, u32[]{:S(2)}, u32[]{:S(2)}) %all-to-all-start) | async-done | bytes 131104 | tf_op jit(solution)/shard_map/all_to_all | solution.py:258
  26.4 0.0 copy-done
  26.5 2.3 %pack.1 = (bf16[16,2560]{1,0:T(8,128)(2,1)S(1)}, f32[16,768]{1,0:T(8,128)S(1)}) custom-call(f32[16,512]{1,0:T(8,128)S(1)} %get-tuple-element.12.cycles_ref, f32[256,128]{1,0:T(8,128)S(1)} %bitcast.13, bf16[2560,256]{1,0:T(8,128)(2,1)S(1)} %bitcast.15, bf16[2560,512]{1,0:T(8,128)(2,1)} %bitcast.19), custom_call_target="tpu_custom_call" | custom-call | flops 30000001024 | bytes 4000000 | tf_op jit(solution)/shard_map/pack/pallas_call | solution.py:275
  28.7 0.0 collective-permute-done.other_ref
  28.7 0.5 sums.1
  29.3 22.9 %all_to_all.10 = f32[256,1,128]{2,1,0:T(1,128)S(1)} all-to-all(f32[256,1,128]{2,1,0:T(1,128)S(1)} %bitcast.11), channel_id=1, replica_groups={{304,308,312,316,320,324,328,332,336,340,344,348,352,356,360,364,368,37..., dimensions={0} | all-to-all | bytes 262144 | tf_op jit(solution)/shard_map/all_to_all | solution.py:302
  52.1 1.3 %fields.1 = f32[3,2,21600]{2,1,0:T(2,128)} custom-call(f32[256,128]{1,0:T(8,128)S(1)} %bitcast.12, bf16[256,512]{1,0:T(8,128)(2,1)S(1)} %get-tuple-element.17.lon_ref, f32[176,256]{1,0:T(8,128)S(1)} %get-tuple-element.18.turns_ref), custom_call_target="tpu_custom_call" | custom-call | tf_op jit(solution)/shard_map/fields/pallas_call | solution.py:306
Async XLA Ops:
  0.0 26.5 %copy-start = (bf16[1,2560,256]{2,1,0:T(8,128)(2,1)S(1)}, bf16[1,2560,256]{2,1,0:T(8,128)(2,1)}, u32[]{:S(2)}) copy-start(bf16[1,2560,256]{2,1,0:T(8,128)(2,1)} %param.6) | copy-start | bytes 3932164
  1.8 24.7 %all-to-all-start = ((f32[128,2,128]{2,1,0:T(2,128)}), f32[128,2,128]{2,1,0:T(2,128)S(1)}, u32[]{:S(2)}, u32[]{:S(2)}) async-start(f32[128,2,128]{2,1,0:T(2,128)} %bitcast.17), calls=%async_computation | async-start | bytes 262144 | tf_op jit(solution)/shard_map/all_to_all | solution.py:258
  22.6 6.1 %collective-permute-start = (bf16[2560,256]{1,0:T(8,128)(2,1)}, bf16[2560,256]{1,0:T(8,128)(2,1)S(1)}, u32[]{:S(2)}, u32[]{:S(2)}) collective-permute-start(bf16[2560,256]{1,0:T(8,128)(2,1)} %bitcast.14), channel_id=1, source_target_pairs={{0,2},{2,0},{1,3},{3,1},{4,6},{6,4},{5,7},{7,5},{8,10},{10,8},{9,1... | collective-permute-start | bytes 3932168 | tf_op jit(solution)/shard_map/ppermute | solution.py:261
  24.5 0.7 %copy-start.1 = (s32[128]{0:T(128)S(1)}, s32[128]{0:T(128)}, u32[]{:S(2)}) copy-start(s32[128]{0:T(128)} %param.5) | copy-start | bytes 1540

commit v5 on v4

--- a/solution.py
+++ b/solution.py
@@ -18,7 +18,7 @@
 INNER = 256
 OUTER = -(-NLON // INNER)
 TURNS = 88
-PARTS = 5
+PARTS = 10
 PART = HALF * LANES // PARTS
 STEP = 22
 FIRST = 76

time: 53.8 us -> 54.8 us (1.019)
  Pallas kernels: 6.45 us -> 7.47 us
    pallas_call x1, Pallas kernels: 2.26 us -> 3.28 us  [on_device(): pl.pallas_call(pack_kernel, out_shape=(jax.ShapeDtypeStruct((16, HALF * L...]
  transfers between devices with their start and end apart: 2 -> 2, of which waited for: 1 -> 1; matrix products, arithmetic and copies ran while one was open for 0% -> 0% of each run, Pallas kernels for 5% -> 7%
where the time goes in v5:
time: 54.8 us; the launch traced here: 54.5 us
  blocking collectives  22.9 us (42%)
  starting transfers between devices  22.7 us (41%)
  Pallas kernels  7.47 us (14%)
  waiting for transfers between devices  0.7 us (1%)
  local copies, waits for them, and re-layouts  0.65 us (1%)
    all_to_all x1, blocking collectives, on_device(): lax.all_to_all(spectra.reshape(2 * PAIRS, 1, LANES), ('band', 'shard'), 0...  22.9 us
    all_to_all x1, starting transfers between devices, on_device(): lax.all_to_all(sent.reshape(PAIRS, 2, LANES), 'shard', 0, 0, axis_index_g...  20.8 us
    pallas_call x1, Pallas kernels, on_device(): pl.pallas_call(pack_kernel, out_shape=(jax.ShapeDtypeStruct((16, HALF * L...  3.28 us
    ppermute x1, starting transfers between devices, on_device(): other = lax.ppermute(own, 'comp', [(0, 1), (1, 0)])  1.92 us
    pallas_call x1, Pallas kernels, on_device(): pl.pallas_call(send_kernel, out_shape=jax.ShapeDtypeStruct((2 * PAIRS, LA...  1.77 us
    pallas_call x1, Pallas kernels, on_device(): pl.pallas_call(field_kernel, out_shape=jax.ShapeDtypeStruct((3, 2, NLON),...  1.33 us
  transfers between devices with their start and end apart: 2, of which 1 were waited for; matrix products, arithmetic and copies ran while one was open for 0% of the time, Pallas kernels for 7%

profile of v5, /device:TPU:2, one launch (start us, length us, event | category | flops | bytes accessed | tf_op | source)
XLA Modules:
  0.0 54.5 jit_solution(17128958222484208472)
XLA Ops:
  0.0 0.0 copy-start
  0.0 1.8 %send.1 = f32[256,128]{1,0:T(8,128)} custom-call(f32[2,40,256]{2,1,0:T(8,128)} %bitcast.18), custom_call_target="tpu_custom_call" | custom-call | tf_op jit(solution)/shard_map/send/pallas_call | solution.py:247
  1.8 20.8 %all-to-all-start = ((f32[128,2,128]{2,1,0:T(2,128)}), f32[128,2,128]{2,1,0:T(2,128)S(1)}, u32[]{:S(2)}, u32[]{:S(2)}) async-start(f32[128,2,128]{2,1,0:T(2,128)} %bitcast.17), calls=%async_computation | async-start | bytes 262144 | tf_op jit(solution)/shard_map/all_to_all | solution.py:258
  22.6 1.9 %collective-permute-start = (bf16[2560,256]{1,0:T(8,128)(2,1)}, bf16[2560,256]{1,0:T(8,128)(2,1)S(1)}, u32[]{:S(2)}, u32[]{:S(2)}) collective-permute-start(bf16[2560,256]{1,0:T(8,128)(2,1)} %bitcast.14), channel_id=1, source_target_pairs={{0,2},{2,0},{1,3},{3,1},{4,6},{6,4},{5,7},{7,5},{8,10},{10,8},{9,1... | collective-permute-start | bytes 3932168 | tf_op jit(solution)/shard_map/ppermute | solution.py:261
  24.5 0.0 copy-start.1
  24.6 0.6 %copy-done.1 = s32[128]{0:T(128)S(1)} copy-done((s32[128]{0:T(128)S(1)}, s32[128]{0:T(128)}, u32[]{:S(2)}) %copy-start.1) | copy-done | bytes 536
  25.2 0.5 %tables.1 = (bf16[256,512]{1,0:T(8,128)(2,1)S(1)}, f32[176,256]{1,0:T(8,128)S(1)}, f32[16,512]{1,0:T(8,128)S(1)}) custom-call(s32[1,128]{1,0:T(1,128)S(1)} %bitcast.16), custom_call_target="tpu_custom_call" | custom-call | flops 400000000 | bytes 600000 | tf_op jit(solution)/shard_map/tables/pallas_call | solution.py:262
  25.7 0.7 %all-to-all-done = f32[128,2,128]{2,1,0:T(2,128)S(1)} async-done(((f32[128,2,128]{2,1,0:T(2,128)}), f32[128,2,128]{2,1,0:T(2,128)S(1)}, u32[]{:S(2)}, u32[]{:S(2)}) %all-to-all-start) | async-done | bytes 131104 | tf_op jit(solution)/shard_map/all_to_all | solution.py:258
  26.4 0.0 copy-done
  26.5 3.3 %pack.1 = (bf16[16,2560]{1,0:T(8,128)(2,1)S(1)}, f32[16,768]{1,0:T(8,128)S(1)}) custom-call(f32[16,512]{1,0:T(8,128)S(1)} %get-tuple-element.12.cycles_ref, f32[256,128]{1,0:T(8,128)S(1)} %bitcast.13, bf16[2560,256]{1,0:T(8,128)(2,1)S(1)} %bitcast.15, bf16[2560,512]{1,0:T(8,128)(2,1)} %bitcast.19), custom_call_target="tpu_custom_call" | custom-call | flops 30000001024 | bytes 4000000 | tf_op jit(solution)/shard_map/pack/pallas_call | solution.py:275
  29.7 0.0 collective-permute-done.other_ref
  29.8 0.5 sums.1
  30.3 22.9 %all_to_all.10 = f32[256,1,128]{2,1,0:T(1,128)S(1)} all-to-all(f32[256,1,128]{2,1,0:T(1,128)S(1)} %bitcast.11), channel_id=1, replica_groups={{304,308,312,316,320,324,328,332,336,340,344,348,352,356,360,364,368,37..., dimensions={0} | all-to-all | bytes 262144 | tf_op jit(solution)/shard_map/all_to_all | solution.py:302
  53.2 1.3 %fields.1 = f32[3,2,21600]{2,1,0:T(2,128)} custom-call(f32[256,128]{1,0:T(8,128)S(1)} %bitcast.12, bf16[256,512]{1,0:T(8,128)(2,1)S(1)} %get-tuple-element.17.lon_ref, f32[176,256]{1,0:T(8,128)S(1)} %get-tuple-element.18.turns_ref), custom_call_target="tpu_custom_call" | custom-call | tf_op jit(solution)/shard_map/fields/pallas_call | solution.py:306
Async XLA Ops:
  0.0 26.5 %copy-start = (bf16[1,2560,256]{2,1,0:T(8,128)(2,1)S(1)}, bf16[1,2560,256]{2,1,0:T(8,128)(2,1)}, u32[]{:S(2)}) copy-start(bf16[1,2560,256]{2,1,0:T(8,128)(2,1)} %param.6) | copy-start | bytes 3932164
  1.8 24.7 %all-to-all-start = ((f32[128,2,128]{2,1,0:T(2,128)}), f32[128,2,128]{2,1,0:T(2,128)S(1)}, u32[]{:S(2)}, u32[]{:S(2)}) async-start(f32[128,2,128]{2,1,0:T(2,128)} %bitcast.17), calls=%async_computation | async-start | bytes 262144 | tf_op jit(solution)/shard_map/all_to_all | solution.py:258
  22.6 7.1 %collective-permute-start = (bf16[2560,256]{1,0:T(8,128)(2,1)}, bf16[2560,256]{1,0:T(8,128)(2,1)S(1)}, u32[]{:S(2)}, u32[]{:S(2)}) collective-permute-start(bf16[2560,256]{1,0:T(8,128)(2,1)} %bitcast.14), channel_id=1, source_target_pairs={{0,2},{2,0},{1,3},{3,1},{4,6},{6,4},{5,7},{7,5},{8,10},{10,8},{9,1... | collective-permute-start | bytes 3932168 | tf_op jit(solution)/shard_map/ppermute | solution.py:261
  24.5 0.7 %copy-start.1 = (s32[128]{0:T(128)S(1)}, s32[128]{0:T(128)}, u32[]{:S(2)}) copy-start(s32[128]{0:T(128)} %param.5) | copy-start | bytes 1540
